TPU v7x, 256 devices: a whole 4x4x8 slice. The times are simulated.
256 devices in a mesh: dp: 8 (over z_hi, x), ctx: 32 (over y, z_lo, core).
Axes of the slice: x: 4, y: 4, z: 8 (z_hi: 2, z_lo: 4; z = z_hi * 4 + z_lo), core: 2. Of those that a mesh axis runs over, the one named last changes fastest.
Arguments:
- inputs: bfloat16 [256, 512, 1536], P('ctx', 'dp'), may hold values from -6 to 6
- cotangent: bfloat16 [256, 512, 1536], P('ctx', 'dp'), may hold values from -6 to 6
- w_in: bfloat16 [1536, 1536], P('dp'), may hold values from -0.15625 to 0.15625
- factor_one: bfloat16 [512, 512], replicated, may hold values from -0.25 to 0.25
- factor_two: bfloat16 [256, 256], replicated, may hold values from -0.375 to 0.375
- kernel: float32 [256, 512], P('ctx'), may hold values from 0.3 to 3
Outputs:
- grad_inputs: bfloat16 [256, 512, 1536], P('ctx', 'dp')
- grad_w_in: float32 [1536, 1536], P('dp')
- grad_one: float32 [512, 512], replicated
- grad_two: float32 [256, 256], replicated
- grad_kernel: float32 [256, 512], P('ctx')
All inputs are finite; a program needn't handle non-finite values.
Results may differ from a plain program's by a relative error of at most 0.0067.
Values may be sent and summed in bfloat16 or wider, within the bound.
No kernel may reach another device: no remote copies, remote signals or barrier semaphores. Data moves between devices by JAX's collectives and lax.ppermute only.
A program may use at most 128 MiB of HBM per device.

v0:
```python
import math

import jax
import jax.numpy as jnp
from jax import lax
from jax.sharding import PartitionSpec as P


def per_device(inputs, cotangent, w_in, factor_one, factor_two, kernel):
    f32 = jnp.float32
    bf16 = jnp.bfloat16
    blocks_dev, pos_dev, width = inputs.shape
    block_len = factor_one.shape[0]
    block_count = factor_two.shape[0]
    tokens_dev = blocks_dev * pos_dev
    rows_in = inputs.reshape(tokens_dev, width)
    whole_w = lax.all_gather(w_in, "dp", axis=0, tiled=True)
    projected = (
        jnp.dot(rows_in, whole_w, preferred_element_type=f32)
        .astype(bf16)
        .reshape(blocks_dev, pos_dev, width)
    )
    grad_mixed = (cotangent.astype(f32) * inputs.astype(f32)).astype(bf16)
    received = lax.all_to_all(projected, "dp", split_axis=2, concat_axis=1, tiled=True)
    inner_part = jnp.einsum("pq,aqc->apc", factor_one, received, preferred_element_type=f32)
    proj_t = received
    scaled = (kernel[:, :, None] * inner_part).astype(bf16)
    received = lax.all_to_all(scaled, "ctx", split_axis=1, concat_axis=0, tiled=True)
    mixed_part = jnp.einsum("ij,jbc->ibc", factor_two, received, preferred_element_type=f32).astype(
        bf16
    )
    grad_mixed_t = lax.all_to_all(
        lax.all_to_all(grad_mixed, "dp", split_axis=2, concat_axis=1, tiled=True),
        "ctx",
        split_axis=1,
        concat_axis=0,
        tiled=True,
    )
    grad_scaled_t = jnp.einsum(
        "ij,ibc->jbc", factor_two, grad_mixed_t, preferred_element_type=f32
    ).astype(bf16)
    two_term = jnp.einsum("ibc,jbc->ij", grad_mixed_t, received, preferred_element_type=f32)
    grad_scaled, mixed_l1 = (
        lax.all_to_all(grad_scaled_t, "ctx", split_axis=0, concat_axis=1, tiled=True),
        lax.all_to_all(mixed_part, "ctx", split_axis=0, concat_axis=1, tiled=True),
    )
    kernel_term = jnp.sum(grad_scaled.astype(f32) * inner_part, axis=2)
    kernel_total = lax.psum(kernel_term, "dp")
    grad_kernel = kernel_total / math.sqrt(width)
    grad_inner = (kernel[:, :, None] * grad_scaled.astype(f32)).astype(bf16)
    one_term = jnp.einsum("apc,aqc->pq", grad_inner, proj_t, preferred_element_type=f32)
    one_total, two_total = lax.psum((one_term, two_term), ("dp", "ctx"))
    grad_one = one_total / math.sqrt(block_count * width)
    grad_two = two_total / math.sqrt(block_len * width)
    grad_proj_l1 = jnp.einsum(
        "pq,apc->aqc", factor_one, grad_inner, preferred_element_type=f32
    ).astype(bf16)
    grad_proj, mixed_home = (
        lax.all_to_all(grad_proj_l1, "dp", split_axis=1, concat_axis=2, tiled=True),
        lax.all_to_all(mixed_l1, "dp", split_axis=1, concat_axis=2, tiled=True),
    )
    grad_rows = grad_proj.reshape(tokens_dev, width)
    mixed_rows = mixed_home.reshape(tokens_dev, width)
    contract_last = (((1,), (1,)), ((), ()))
    back = lax.dot_general(grad_rows, whole_w, contract_last, preferred_element_type=f32)
    cot_rows = cotangent.reshape(tokens_dev, width)
    grad_in = (
        (back + cot_rows.astype(f32) * mixed_rows.astype(f32))
        .astype(bf16)
        .reshape(blocks_dev, pos_dev, width)
    )
    owned = lax.psum_scatter(
        lax.dot_general(rows_in, grad_rows, (((0,), (0,)), ((), ())), preferred_element_type=f32),
        ("dp", "ctx"),
        scatter_dimension=0,
        tiled=True,
    )
    win_total = lax.all_gather(owned, "ctx", axis=0, tiled=True)
    grad_w_in = win_total / math.sqrt(block_count * block_len)
    return (grad_in, grad_w_in, grad_one, grad_two, grad_kernel)


def solution(mesh):
    return jax.shard_map(
        per_device,
        mesh=mesh,
        in_specs=(
            P("ctx", "dp", None),
            P("ctx", "dp", None),
            P("dp", None),
            P(),
            P(),
            P("ctx", None),
        ),
        out_specs=(P("ctx", "dp", None), P("dp", None), P(), P(), P("ctx", None)),
        check_vma=False,
    )
```

profile of v0, /device:TPU:1, one launch (start us, length us, event | category | flops | bytes accessed | tf_op | source)
XLA Modules:
  0.0 842.4 jit_solution(5495628088152820268)
XLA Ops:
  13.0 6.9 reshape.63
  20.0 11.5 %all-to-all-start = ((bf16[8,2,49152]{2,1,0:T(2,128)(2,1)}), bf16[8,2,49152]{2,1,0:T(2,128)(2,1)S(1)}, u32[]{:S(2)}, u32[]{:S(2)}) async-start(bf16[8,2,49152]{2,1,0:T(2,128)(2,1)} %reshape.63), calls=%async_computation | async-start | bytes 3145728 | tf_op jit(solution)/shard_map/all_to_all | solution.py:33
  32.2 24.7 %all-to-all-done = bf16[8,2,49152]{2,1,0:T(2,128)(2,1)S(1)} async-done(((bf16[8,2,49152]{2,1,0:T(2,128)(2,1)}), bf16[8,2,49152]{2,1,0:T(2,128)(2,1)S(1)}, u32[]{:S(2)}, u32[]{:S(2)}) %all-to-all-start) | async-done | bytes 1572896 | tf_op jit(solution)/shard_map/all_to_all | solution.py:33
  66.0 133.0 %all_to_all.123 = bf16[8,512,192]{2,0,1:T(8,128)(2,1)S(1)} all-to-all(bf16[8,512,192]{2,0,1:T(8,128)(2,1)S(1)} %bitcast.109), channel_id=1, replica_groups=mesh['dp'=8,'ctx'=32] {'ctx'}, dimensions={1} | all-to-all | bytes 3145728 | tf_op jit(solution)/shard_map/all_to_all | solution.py:32
  212.2 6.6 convolution_convert_fusion
  218.8 4.9 copy.110
  223.7 6.9 reshape.61
  230.6 31.4 %all-to-all-done.2 = bf16[256,16,192]{2,1,0:T(8,128)(2,1)S(1)} async-done(((bf16[256,16,192]{2,1,0:T(8,128)(2,1)}), bf16[256,16,192]{2,1,0:T(8,128)(2,1)S(1)}, u32[]{:S(2)}, u32[]{:S(2)}) %all-to-all-start.2) | async-done | bytes 1572896 | tf_op jit(solution)/shard_map/all_to_all | solution.py:44
  270.1 5.2 copy.106
  283.8 18.7 %all-to-all-done.4 = bf16[8,2,49152]{2,1,0:T(2,128)(2,1)} async-done(((bf16[8,2,49152]{2,1,0:T(2,128)(2,1)}), bf16[8,2,49152]{2,1,0:T(2,128)(2,1)}, u32[]{:S(2)}, u32[]{:S(2)}) %all-to-all-start.4) | async-done | bytes 1572896 | tf_op jit(solution)/shard_map/all_to_all | solution.py:24
  302.4 8.2 all-to-all-start.3
  310.6 6.7 reshape.62
  317.3 5.0 copy.112
  322.3 5.1 fusion.1
  331.8 21.4 %all-to-all-done.3 = bf16[8,512,192]{2,0,1:T(8,128)(2,1)} async-done(((bf16[8,512,192]{2,0,1:T(8,128)(2,1)}), bf16[8,512,192]{2,0,1:T(8,128)(2,1)}, u32[]{:S(2)}, u32[]{:S(2)}) %all-to-all-start.3) | async-done | bytes 1572896 | tf_op jit(solution)/shard_map/all_to_all | solution.py:59
  353.3 13.1 %all-to-all-start.5 = ((bf16[8,512,192]{2,0,1:T(8,128)(2,1)}), bf16[8,512,192]{2,0,1:T(8,128)(2,1)}, u32[]{:S(2)}, u32[]{:S(2)}) async-start(bf16[8,512,192]{2,0,1:T(8,128)(2,1)} %copy.114), calls=%async_computation.5 | async-start | bytes 4194304 | tf_op jit(solution)/shard_map/all_to_all | solution.py:28
  376.8 8.2 convolution_bitcast_fusion
  385.0 31.2 %all-to-all-done.5 = bf16[8,512,192]{2,0,1:T(8,128)(2,1)} async-done(((bf16[8,512,192]{2,0,1:T(8,128)(2,1)}), bf16[8,512,192]{2,0,1:T(8,128)(2,1)}, u32[]{:S(2)}, u32[]{:S(2)}) %all-to-all-start.5) | async-done | bytes 1572896 | tf_op jit(solution)/shard_map/all_to_all | solution.py:28
  431.0 65.5 %all_to_all.124 = bf16[256,16,192]{2,1,0:T(8,128)(2,1)S(1)} all-to-all(bf16[256,16,192]{2,1,0:T(8,128)(2,1)S(1)} %copy.118), channel_id=1, replica_groups=mesh['dp'=8,'ctx'=32] {'ctx'}, dimensions={0} | all-to-all | bytes 3145728 | tf_op jit(solution)/shard_map/all_to_all | solution.py:45
  503.3 89.8 %psum.23 = f32[8,512]{1,0:T(8,128)S(1)} all-reduce(f32[8,512]{1,0:T(8,128)S(1)} %get-tuple-element.8), channel_id=1, replica_groups=mesh['dp'=8,'ctx'=32] {'dp'}, use_global_device_ids=true, to_apply=%region_4.0 | all-reduce | flops 4096 | bytes 32768 | tf_op jit(solution)/shard_map/psum | solution.py:48
  593.7 176.6 %all-reduce.4.cloned.1.call-done = (f32[1536,1536]{0,1:T(8,128)}, f32[512,512]{1,0:T(8,128)}, f32[256,256]{1,0:T(8,128)}) async-done(((f32[1536,1536]{0,1:T(8,128)}, f32[512,512]{1,0:T(8,128)}, f32[256,256]{1,0:T(8,128)}), (f32[1536,1536]{0,1:T(8,128)}, f32[512,512]{1,0:T(8,128)}, f32[256,256]{1,0:T(8,128)})) %all-reduce.4.cloned.1.call-update) | async-done | bytes 10747920
  781.3 5.3 reshape.47
  789.1 6.1 fusion.2
  795.2 37.8 %all-gather.6.cloned.1.call-done = f32[32,6,1536]{2,1,0:T(8,128)} async-done(((f32[1,6,1536]{2,1,0:T(8,128)}), f32[32,6,1536]{2,1,0:T(8,128)}) %all-gather.6.cloned.1.call-update) | async-done | bytes 1179664 | tf_op jit(solution)/shard_map/all_gather | solution.py:78
  (67 shorter events, 98.6 us)
Async XLA Ops:
  7.2 268.2 %copy-start = (bf16[512,512]{1,0:T(8,128)(2,1)S(1)}, bf16[512,512]{1,0:T(8,128)(2,1)}, u32[]{:S(2)}) copy-start(bf16[512,512]{1,0:T(8,128)(2,1)} %param.9) | copy-start | bytes 1572868
  20.0 36.9 %all-to-all-start = ((bf16[8,2,49152]{2,1,0:T(2,128)(2,1)}), bf16[8,2,49152]{2,1,0:T(2,128)(2,1)S(1)}, u32[]{:S(2)}, u32[]{:S(2)}) async-start(bf16[8,2,49152]{2,1,0:T(2,128)(2,1)} %reshape.63), calls=%async_computation | async-start | bytes 3145728 | tf_op jit(solution)/shard_map/all_to_all | solution.py:33
  31.4 180.8 %all-gather.4.cloned.1.call-start = ((), (), s32[]{:S(2)}) async-start(), calls=%async_computation.8 | async-start | bytes 5308416 | tf_op jit(solution)/shard_map/all_gather | solution.py:17
  199.6 2.8 copy-start.6
  207.5 54.6 %all-to-all-start.2 = ((bf16[256,16,192]{2,1,0:T(8,128)(2,1)}), bf16[256,16,192]{2,1,0:T(8,128)(2,1)S(1)}, u32[]{:S(2)}, u32[]{:S(2)}) async-start(bf16[256,16,192]{2,1,0:T(8,128)(2,1)} %copy.104), calls=%async_computation.2 | async-start | bytes 4194304 | tf_op jit(solution)/shard_map/all_to_all | solution.py:44
  262.1 40.3 %all-to-all-start.4 = ((bf16[8,2,49152]{2,1,0:T(2,128)(2,1)}), bf16[8,2,49152]{2,1,0:T(2,128)(2,1)}, u32[]{:S(2)}, u32[]{:S(2)}) async-start(bf16[8,2,49152]{2,1,0:T(2,128)(2,1)} %reshape.61), calls=%async_computation.4 | async-start | bytes 3145728 | tf_op jit(solution)/shard_map/all_to_all | solution.py:24
  270.1 5.2 copy-start.8
  302.4 50.9 %all-to-all-start.3 = ((bf16[8,512,192]{2,0,1:T(8,128)(2,1)}), bf16[8,512,192]{2,0,1:T(8,128)(2,1)}, u32[]{:S(2)}, u32[]{:S(2)}) async-start(bf16[8,512,192]{2,0,1:T(8,128)(2,1)} %copy.107), calls=%async_computation.3 | async-start | bytes 4194304 | tf_op jit(solution)/shard_map/all_to_all | solution.py:59
  353.3 62.9 %all-to-all-start.5 = ((bf16[8,512,192]{2,0,1:T(8,128)(2,1)}), bf16[8,512,192]{2,0,1:T(8,128)(2,1)}, u32[]{:S(2)}, u32[]{:S(2)}) async-start(bf16[8,512,192]{2,0,1:T(8,128)(2,1)} %copy.114), calls=%async_computation.5 | async-start | bytes 4194304 | tf_op jit(solution)/shard_map/all_to_all | solution.py:28
  366.4 403.9 %all-reduce.4.cloned.1.call-start = ((), (), s32[]{:S(2)}) async-start(), calls=%async_computation.10 | async-start | bytes 21495808
  367.4 1.6 copy-start.2
  424.6 1.4 copy-start.3
  499.2 276.8 %all-to-all-start.7 = ((bf16[8,512,192]{2,0,1:T(8,128)(2,1)}), bf16[8,512,192]{2,0,1:T(8,128)(2,1)S(1)}, u32[]{:S(2)}, u32[]{:S(2)}) async-start(bf16[8,512,192]{2,0,1:T(8,128)(2,1)} %copy.120), calls=%async_computation.7 | async-start | bytes 4194304 | tf_op jit(solution)/shard_map/all_to_all | solution.py:60
  503.3 329.8 %all-gather.6.cloned.1.call-start = ((), (), s32[]{:S(2)}) async-start(), calls=%async_computation.9 | async-start | bytes 1622016 | tf_op jit(solution)/shard_map/all_gather | solution.py:78
  770.3 2.6 copy-start.7
  781.3 5.3 copy-start.4
  786.6 2.5 copy-start.5
  833.1 2.9 copy-start.1
Sparse Core Ops, SparseCore 0:
  34.9 157.1 all-gather.3
  424.7 345.5 all-reduce.3
  773.1 59.9 all-gather.5
where the time goes:
time: 844 us; the launch traced here: 842 us
  waiting for transfers between devices  343 us (41%)
  blocking collectives  288 us (34%)
  local copies, waits for them, and re-layouts  100 us (12%)
  starting transfers between devices  46.5 us (6%)
  matrix products  39.2 us (5%)
  between operations  14 us (2%)
  other arithmetic  12 us (1%)
    unnamed x4, waiting for transfers between devices  177 us
    all_to_all x1, blocking collectives, per_device(): lax.all_to_all(lax.all_to_all(grad_mixed, 'dp', split_axis=2, concat_axis...  133 us
    psum x1, blocking collectives, per_device(): kernel_total = lax.psum(kernel_term, 'dp')  89.8 us
    all_to_all x1, blocking collectives, per_device(): lax.all_to_all(mixed_part, 'ctx', split_axis=0, concat_axis=1, tiled=True)  65.5 us
    all_gather x1, waiting for transfers between devices, per_device(): win_total = lax.all_gather(owned, 'ctx', axis=0, tiled=True)  37.8 us
    all_to_all x1, waiting for transfers between devices, per_device(): lax.all_to_all(grad_scaled_t, 'ctx', split_axis=0, concat_axis=1, tiled=T...  31.4 us
    all_to_all x1, waiting for transfers between devices, per_device(): lax.all_to_all(scaled, 'ctx', split_axis=1, concat_axis=0, tiled=True)  31.2 us
    unnamed x24, local copies, waits for them, and re-layouts  30.5 us
  transfers between devices with their start and end apart: 9, of which 7 were waited for; matrix products, arithmetic and copies ran while one was open for 15% of the time, Pallas kernels for 0%

commit v1 on v0

v1 whole, which is shorter than its diff:
```python
import math

import jax
import jax.numpy as jnp
from jax import lax
from jax.sharding import Mesh
from jax.sharding import PartitionSpec as P

F32 = jnp.float32
BF16 = jnp.bfloat16
ALL = ("zh", "x", "y", "zl", "c")
DP = ("zh", "x")
CTX = ("y", "zl", "c")


def exchange(array, axes):
    return lax.all_to_all(array, axes, 0, 0, tiled=True)


def gather_w(w_in):
    rows, width = w_in.shape
    piece = rows // 8
    place = lax.axis_index("y") * 2 + lax.axis_index("c")
    mine = lax.dynamic_slice_in_dim(w_in, place * piece, piece, 0)
    other = lax.ppermute(mine, "zh", [(0, 1), (1, 0)])
    low = lax.axis_index("zh") == 0
    both = jnp.concatenate([jnp.where(low, mine, other), jnp.where(low, other, mine)], 0)
    whole = lax.all_gather(both, ("x", "y", "c"), axis=0, tiled=True)
    whole = whole.reshape(4, 8, 2, piece, width).transpose(2, 0, 1, 3, 4)
    return whole.reshape(8 * rows, width)


def per_device(inputs, cotangent, w_in, factor_one, factor_two, kernel):
    blocks, pos, width = inputs.shape
    tokens = blocks * pos
    devices = 256
    chans = width // devices
    block_len = factor_one.shape[0]
    block_count = factor_two.shape[0]

    def to_channels(array_t):
        send = array_t.reshape(chans, devices, tokens).transpose(1, 0, 2)
        got = exchange(send.reshape(devices, -1, 128), ALL)
        got = got.reshape(8, 32, chans, blocks, pos).transpose(2, 1, 3, 0, 4)
        return got.reshape(chans, block_count, block_len)

    def to_home(array):
        send = array.reshape(chans, 32, blocks, 8, pos).transpose(3, 1, 0, 2, 4)
        got = exchange(send.reshape(devices, -1, 128), ALL)
        got = got.reshape(devices, chans, tokens).transpose(1, 0, 2)
        return got.reshape(width, tokens)

    rows_in = inputs.reshape(tokens, width)
    cot_rows = cotangent.reshape(tokens, width)
    xc = to_channels(rows_in.T)
    whole_w = gather_w(w_in)
    scale = lax.all_gather(kernel, CTX, axis=0, tiled=True)
    grad_mixed = (cot_rows.astype(F32) * rows_in.astype(F32)).astype(BF16)
    yc = jnp.einsum("jaq,pq->jap", xc, factor_one, preferred_element_type=F32)
    sc = (scale[None] * yc).astype(BF16)
    mc = jnp.einsum("il,jlp->jip", factor_two, sc, preferred_element_type=F32).astype(BF16)
    mixed_t = to_home(mc)
    ht = lax.dot_general(
        whole_w, grad_mixed, (((1,), (1,)), ((), ())), preferred_element_type=F32
    ).astype(BF16)
    hc = to_channels(ht)
    uc = jnp.einsum("il,jip->jlp", factor_two, hc, preferred_element_type=F32)
    kernel_term = jnp.sum(uc * yc, axis=0)
    tc = (scale[None] * uc).astype(BF16)
    back_c = jnp.einsum("jap,pq->jaq", tc, factor_one, preferred_element_type=F32).astype(BF16)
    back_t = to_home(back_c)
    one_term = jnp.einsum("jap,jaq->pq", tc, xc, preferred_element_type=F32)
    two_term = jnp.einsum("jip,jlp->il", hc, sc, preferred_element_type=F32)
    win_term = jnp.dot(mixed_t, grad_mixed, preferred_element_type=F32)

    extra = jnp.concatenate(
        [
            one_term.reshape(devices, -1),
            two_term.reshape(devices, -1),
            kernel_term.reshape(32, blocks, 8, pos).transpose(2, 0, 1, 3).reshape(devices, -1),
        ],
        1,
    ).astype(BF16)
    pieces = jnp.concatenate([win_term.astype(BF16).reshape(devices, -1), extra], 1)
    lines = pieces.shape[1] // 128
    pieces = pieces.reshape(2, 4, 4, 4, 2, lines, 128).transpose(4, 0, 1, 2, 3, 5, 6)
    got = exchange(pieces.reshape(-1, 128), ("c",)).reshape(2, -1, 128)
    part = (got[0].astype(F32) + got[1].astype(F32)).astype(BF16)
    part = part.reshape(2, 16, 4, lines, 128).transpose(1, 0, 2, 3, 4)
    got = exchange(part.reshape(-1, 128), ("x", "y")).reshape(16, -1, 128)
    part = jnp.sum(got.astype(F32), 0).astype(BF16)
    got = exchange(part, ("zh", "zl")).reshape(8, lines, 128)
    part = jnp.sum(got.astype(F32), 0)

    win_lines = width * width // devices // 128
    small = part[win_lines:].astype(BF16)
    small = exchange(jnp.broadcast_to(small[None], (8,) + small.shape), DP)
    one_two = small[:, :10]
    mine = jnp.concatenate([part[:win_lines].astype(BF16), one_two.reshape(-1, 128)], 0)
    got = exchange(jnp.broadcast_to(mine[None], (32,) + mine.shape), CTX)
    win_total = got[:, :win_lines].astype(F32).reshape(width // 8, width)
    one_two = got[:, win_lines:].reshape(32, 8, 10, 128).transpose(1, 0, 2, 3)
    one_total = one_two[:, :, :8].astype(F32).reshape(block_len, block_len)
    two_total = one_two[:, :, 8:].astype(F32).reshape(block_count, block_count)
    kernel_total = small[:, 10:].astype(F32).reshape(8, blocks, pos).transpose(1, 0, 2)
    grad_kernel = kernel_total.reshape(blocks, block_len) / math.sqrt(width)
    grad_one = one_total / math.sqrt(block_count * width)
    grad_two = two_total / math.sqrt(block_len * width)
    grad_w_in = win_total / math.sqrt(block_count * block_len)

    mixed = lax.dot_general(
        mixed_t, whole_w, (((0,), (0,)), ((), ())), preferred_element_type=F32
    ).astype(BF16)
    grad_in = back_t.T.astype(F32) + cot_rows.astype(F32) * mixed.astype(F32)
    grad_in = grad_in.astype(BF16).reshape(blocks, pos, width)
    return (grad_in, grad_w_in, grad_one, grad_two, grad_kernel)


def solution(mesh):
    fine = Mesh(mesh.devices.reshape(2, 4, 4, 4, 2), ALL)
    return jax.shard_map(
        per_device,
        mesh=fine,
        in_specs=(
            P(CTX, DP, None),
            P(CTX, DP, None),
            P(DP, None),
            P(),
            P(),
            P(CTX, None),
        ),
        out_specs=(P(CTX, DP, None), P(DP, None), P(), P(), P(CTX, None)),
        check_vma=False,
    )
```

time: 844 us -> 550 us (0.65)
  waiting for transfers between devices: 343 us -> 126 us
  blocking collectives: 288 us -> 132 us
  local copies, waits for them, and re-layouts: 100 us -> 151 us
  starting transfers between devices: 46.5 us -> 68.9 us
    unnamed x4 -> x1, waiting for transfers between devices: 177 us -> 0.02 us
    all_to_all x2 -> x3, blocking collectives: 198 us -> 60 us  [exchange(): return lax.all_to_all(array, axes, 0, 0, tiled=True)]
    psum x1 -> x0, blocking collectives: 89.8 us -> none  [per_device(): kernel_total = lax.psum(kernel_term, 'dp')]
    all_gather x0 -> x1, blocking collectives: none -> 71.5 us  [per_device(): scale = lax.all_gather(kernel, CTX, axis=0, tiled=True)]
    reshape x2 -> x18, local copies, waits for them, and re-layouts: 7.67 us -> 70.5 us  [the longest x3 14.2 us: to_home(): send = array.reshape(chans, 32, blocks, 8, pos).transpose(3, 1, 0, 2, 4)]
    all_to_all x6, waiting for transfers between devices: 127 us -> 85.5 us  [exchange(): return lax.all_to_all(array, axes, 0, 0, tiled=True)]
    transpose x0 -> x10, local copies, waits for them, and re-layouts: none -> 35.9 us  [the longest x2 14.4 us: to_channels(): got = got.reshape(8, 32, chans, blocks, pos).transpose(2, 1, 3, 0, 4)]
    unnamed x24, local copies, waits for them, and re-layouts: 30.5 us -> 3.98 us
  transfers between devices with their start and end apart: 9 -> 8, of which waited for: 7 -> 5; matrix products, arithmetic and copies ran while one was open for 15% -> 16% of each run, Pallas kernels for 0% -> 0%
where the time goes in v1:
time: 550 us; the launch traced here: 542 us
  local copies, waits for them, and re-layouts  151 us (27%)
  blocking collectives  132 us (24%)
  waiting for transfers between devices  126 us (23%)
  starting transfers between devices  68.9 us (13%)
  matrix products  31.4 us (6%)
  other arithmetic  17.5 us (3%)
  between operations  14.9 us (3%)
    all_to_all x6, waiting for transfers between devices, exchange(): return lax.all_to_all(array, axes, 0, 0, tiled=True)  85.5 us
    all_gather x1, blocking collectives, per_device(): scale = lax.all_gather(kernel, CTX, axis=0, tiled=True)  71.5 us
    all_to_all x6, starting transfers between devices, exchange(): return lax.all_to_all(array, axes, 0, 0, tiled=True)  61.1 us
    all_to_all x3, blocking collectives, exchange(): return lax.all_to_all(array, axes, 0, 0, tiled=True)  60 us
    all_gather x1, waiting for transfers between devices, gather_w(): whole = lax.all_gather(both, ('x', 'y', 'c'), axis=0, tiled=True)  39.1 us
    transpose x2, local copies, waits for them, and re-layouts, to_channels(): got = got.reshape(8, 32, chans, blocks, pos).transpose(2, 1, 3, 0, 4)  14.4 us
    reshape x3, local copies, waits for them, and re-layouts, to_home(): send = array.reshape(chans, 32, blocks, 8, pos).transpose(3, 1, 0, 2, 4)  14.2 us
    all_to_all x4, local copies, waits for them, and re-layouts, exchange(): return lax.all_to_all(array, axes, 0, 0, tiled=True)  12.8 us
  transfers between devices with their start and end apart: 8, of which 5 were waited for; matrix products, arithmetic and copies ran while one was open for 16% of the time, Pallas kernels for 0%

profile of v1, /device:TPU:1, one launch (start us, length us, event | category | flops | bytes accessed | tf_op | source)
XLA Modules:
  0.0 542.2 jit_solution(10374302185697039439)
XLA Ops:
  8.2 7.7 %collective-permute-start = (bf16[24,1536]{1,0:T(8,128)(2,1)S(1)}, bf16[24,1536]{1,0:T(8,128)(2,1)S(1)}, u32[]{:S(2)}, u32[]{:S(2)}) collective-permute-start(bf16[24,1536]{1,0:T(8,128)(2,1)S(1)} %constant_dynamic-slice_fusion), channel_id=1, source_target_pairs={{0,128},{128,0},{1,129},{129,1},{2,130},{130,2},{3,131},{131,3},{4... | collective-permute-start | bytes 221192 | tf_op jit(solution)/shard_map/ppermute | solution.py:25
  25.6 16.3 %all-to-all-start.2 = ((bf16[256,24,128]{2,1,0:T(8,128)(2,1)}), bf16[256,24,128]{2,1,0:T(8,128)(2,1)}, u32[]{:S(2)}, u32[]{:S(2)}) async-start(bf16[256,24,128]{2,1,0:T(8,128)(2,1)} %copy.85), calls=%async_computation.2 | async-start | bytes 3145728 | tf_op jit(solution)/shard_map/all_to_all | solution.py:17
  44.9 39.1 %all-gather.2.cloned.1.call-done = bf16[1536,1536]{1,0:T(8,128)(2,1)} async-done(((bf16[48,1536]{1,0:T(8,128)(2,1)}), bf16[1536,1536]{1,0:T(8,128)(2,1)}) %all-gather.2.cloned.1.call-update) | async-done | bytes 4718608 | tf_op jit(solution)/shard_map/all_gather | solution.py:28
  94.4 9.9 %all-to-all-start = ((bf16[256,24,128]{2,1,0:T(8,128)(2,1)}), bf16[256,24,128]{2,1,0:T(8,128)(2,1)S(1)}, u32[]{:S(2)}, u32[]{:S(2)}) async-start(bf16[256,24,128]{2,1,0:T(8,128)(2,1)} %copy.75), calls=%async_computation | async-start | bytes 3145728 | tf_op jit(solution)/shard_map/all_to_all | solution.py:17
  104.4 71.5 %all_gather.6 = f32[256,512]{1,0:T(8,128)S(1)} all-gather(f32[8,512]{1,0:T(8,128)S(1)} %copy-done.10), channel_id=1, replica_groups=mesh['zh'=2,'x'=4,'y'=4,'zl'=4,'c'=2] {'y','zl','c'}, dimensions={0}, use_global_device_ids=true | all-gather | bytes 540672 | tf_op jit(solution)/shard_map/all_gather | solution.py:57
  176.1 5.3 reshape.158
  181.4 7.2 %copy.86 = bf16[6,32,8,8,64]{4,3,2,1,0:T(8,128)(2,1)} copy(bf16[6,32,8,8,64]{4,2,0,1,3:T(8,128)(2,1)} %bitcast.111) | data formatting | bytes 3145728 | tf_op jit(solution)/shard_map/transpose | solution.py:44
  188.6 5.4 reshape.159
  196.9 7.2 %copy.76 = bf16[6,32,8,8,64]{4,3,2,1,0:T(8,128)(2,1)} copy(bf16[6,32,8,8,64]{4,2,0,1,3:T(8,128)(2,1)} %bitcast.112) | data formatting | bytes 3145728 | tf_op jit(solution)/shard_map/transpose | solution.py:44
  232.4 11.4 %all-to-all-start.3 = ((bf16[256,24,128]{2,1,0:T(8,128)(2,1)}), bf16[256,24,128]{2,1,0:T(8,128)(2,1)}, u32[]{:S(2)}, u32[]{:S(2)}) async-start(bf16[256,24,128]{2,1,0:T(8,128)(2,1)} %reshape.161), calls=%async_computation.3 | async-start | bytes 3145728 | tf_op jit(solution)/shard_map/all_to_all | solution.py:17
  255.0 30.3 %all-to-all-done.3 = bf16[256,24,128]{2,1,0:T(8,128)(2,1)} async-done(((bf16[256,24,128]{2,1,0:T(8,128)(2,1)}), bf16[256,24,128]{2,1,0:T(8,128)(2,1)}, u32[]{:S(2)}, u32[]{:S(2)}) %all-to-all-start.3) | async-done | bytes 1572896 | tf_op jit(solution)/shard_map/all_to_all | solution.py:17
  289.8 5.7 %convolution_convert_fusion = bf16[1536,1536]{1,0:T(8,128)(2,1)} fusion(bf16[1536,512]{1,0:T(8,128)(2,1)S(1)} %bitcast.109, bf16[512,1536]{1,0:T(8,128)(2,1)} %bitcast.130), kind=kOutput, calls=%fused_computation | convolution fusion | flops 2418278400 | bytes 7864320 | tf_op jit(solution)/shard_map/dot_general | solution.py:74
  295.5 9.4 %reshape.165 = bf16[256,9216]{1,0:T(8,128)(2,1)} reshape(bf16[1536,1536]{1,0:T(8,128)(2,1)} %convolution_convert_fusion) | data formatting | bytes 9437184 | tf_op jit(solution)/shard_map/reshape | solution.py:84
  305.0 6.9 %pad_maximum_fusion = bf16[256,11008]{1,0:T(8,128)(2,1)} fusion(bf16[256,512]{1,0:T(8,128)(2,1)S(1)} %reshape.168, bf16[256,256]{1,0:T(8,128)(2,1)S(1)} %copy.96, bf16[256,1024]{1,0:T(8,128)(2,1)S(1)} %reshape.166, bf16[256,9216]{1,0:T(8,128)(2,1)} %reshape.165), kind=kLoop, calls=%fused_computation.1 | loop fusion | flops 22544384 | bytes 11272192 | tf_op jit(solution)/shard_map/concatenate | solution.py:84
  311.8 9.9 %reshape.169 = bf16[2,4,4,4,2,86,128]{6,5,4,3,2,1,0:T(8,128)(2,1)} reshape(bf16[256,11008]{1,0:T(8,128)(2,1)} %pad_maximum_fusion) | data formatting | bytes 11272192 | tf_op jit(solution)/shard_map/reshape | solution.py:86
  321.8 6.6 %copy.97 = bf16[2,2,4,4,4,86,128]{6,5,4,3,2,1,0:T(8,128)(2,1)} copy(bf16[2,2,4,4,4,86,128]{6,5,0,4,3,2,1:T(8,128)(2,1)} %bitcast.108) | data formatting | bytes 11272192 | tf_op jit(solution)/shard_map/transpose | solution.py:86
  328.4 9.2 %all_to_all.40 = bf16[2,11008,128]{2,1,0:T(8,128)(2,1)} reshape(bf16[2,2,4,4,4,86,128]{6,5,4,3,2,1,0:T(8,128)(2,1)} %copy.97) | data formatting | bytes 11272192 | tf_op jit(solution)/shard_map/all_to_all | solution.py:17
  337.6 9.6 %all_to_all.57 = bf16[2,11008,128]{2,1,0:T(8,128)(2,1)S(1)} all-to-all(bf16[2,11008,128]{2,1,0:T(8,128)(2,1)} %all_to_all.40), channel_id=1, replica_groups=mesh['zh'=2,'x'=4,'y'=4,'zl'=4,'c'=2] {'c'}, dimensions={0} | all-to-all | bytes 11272192 | tf_op jit(solution)/shard_map/all_to_all | solution.py:17
  358.0 39.5 %all_to_all.58 = bf16[16,688,128]{2,1,0:T(8,128)(2,1)} all-to-all(bf16[16,688,128]{2,1,0:T(8,128)(2,1)S(1)} %copy.99), channel_id=1, replica_groups=mesh['zh'=2,'x'=4,'y'=4,'zl'=4,'c'=2] {'x','y'}, dimensions={0} | all-to-all | bytes 5636096 | tf_op jit(solution)/shard_map/all_to_all | solution.py:17
  399.8 11.0 %all_to_all.59 = bf16[8,86,128]{2,1,0:T(8,128)(2,1)S(1)} all-to-all(bf16[8,86,128]{2,1,0:T(8,128)(2,1)S(1)} %all_to_all.44), channel_id=1, replica_groups=mesh['zh'=2,'x'=4,'y'=4,'zl'=4,'c'=2] {'zh','zl'}, dimensions={0} | all-to-all | bytes 352256 | tf_op jit(solution)/shard_map/all_to_all | solution.py:17
  433.2 15.1 %all-to-all-start.1 = ((bf16[256,24,128]{2,1,0:T(8,128)(2,1)}), bf16[256,24,128]{2,1,0:T(8,128)(2,1)}, u32[]{:S(2)}, u32[]{:S(2)}) async-start(bf16[256,24,128]{2,1,0:T(8,128)(2,1)} %reshape.154), calls=%async_computation.1 | async-start | bytes 3145728 | tf_op jit(solution)/shard_map/all_to_all | solution.py:17
  448.4 41.4 %all-to-all-done.1 = bf16[256,24,128]{2,1,0:T(8,128)(2,1)} async-done(((bf16[256,24,128]{2,1,0:T(8,128)(2,1)}), bf16[256,24,128]{2,1,0:T(8,128)(2,1)}, u32[]{:S(2)}, u32[]{:S(2)}) %all-to-all-start.1) | async-done | bytes 1572896 | tf_op jit(solution)/shard_map/all_to_all | solution.py:17
  506.5 6.8 %fusion.1 = bf16[512,1536]{1,0:T(8,128)(2,1)} fusion(f32[1536,512]{0,1:T(8,128)} %copy.82, bf16[1536,512]{1,0:T(8,128)(2,1)S(1)} %bitcast.110, bf16[1536,1536]{1,0:T(8,128)(2,1)} %bitcast.107, bf16[8,64,1536]{2,1,0:T(8,128)(2,1)} %param.7), kind=kOutput, calls=%fused_computation.5 | convolution fusion | flops 2420637696 | bytes 12582912 | tf_op jit(solution)/shard_map/dot_general | solution.py:111
  514.0 13.9 %all-to-all-done.8 = bf16[32,152,128]{2,1,0:T(8,128)(2,1)S(1)} async-done(((bf16[32,152,128]{2,1,0:T(8,128)(2,1)}), bf16[32,152,128]{2,1,0:T(8,128)(2,1)S(1)}, u32[]{:S(2)}, u32[]{:S(2)}) %all-to-all-start.8) | async-done | bytes 1245216 | tf_op jit(solution)/shard_map/all_to_all | solution.py:17
  (95 shorter events, 131.0 us)
Async XLA Ops:
  7.2 202.1 %copy-start = (bf16[512,512]{1,0:T(8,128)(2,1)S(1)}, bf16[512,512]{1,0:T(8,128)(2,1)}, u32[]{:S(2)}) copy-start(bf16[512,512]{1,0:T(8,128)(2,1)} %param.9) | copy-start | bytes 1572868
  7.2 76.8 %all-gather.2.cloned.1.call-start = ((), (), s32[]{:S(2)}) async-start(), calls=%async_computation.9 | async-start | bytes 4866048 | tf_op jit(solution)/shard_map/all_gather | solution.py:28
  8.2 9.6 %collective-permute-start = (bf16[24,1536]{1,0:T(8,128)(2,1)S(1)}, bf16[24,1536]{1,0:T(8,128)(2,1)S(1)}, u32[]{:S(2)}, u32[]{:S(2)}) collective-permute-start(bf16[24,1536]{1,0:T(8,128)(2,1)S(1)} %constant_dynamic-slice_fusion), channel_id=1, source_target_pairs={{0,128},{128,0},{1,129},{129,1},{2,130},{130,2},{3,131},{131,3},{4... | collective-permute-start | bytes 221192 | tf_op jit(solution)/shard_map/ppermute | solution.py:25
  22.7 19.3 %copy-start.5 = (bf16[8,64,1536]{2,1,0:T(8,128)(2,1)S(1)}, bf16[8,64,1536]{2,1,0:T(8,128)(2,1)}, u32[]{:S(2)}) copy-start(bf16[8,64,1536]{2,1,0:T(8,128)(2,1)} %param.7) | copy-start | bytes 4718596
  25.6 68.8 %all-to-all-start.2 = ((bf16[256,24,128]{2,1,0:T(8,128)(2,1)}), bf16[256,24,128]{2,1,0:T(8,128)(2,1)}, u32[]{:S(2)}, u32[]{:S(2)}) async-start(bf16[256,24,128]{2,1,0:T(8,128)(2,1)} %copy.85), calls=%async_computation.2 | async-start | bytes 3145728 | tf_op jit(solution)/shard_map/all_to_all | solution.py:17
  84.0 2.9 copy-start.7
  86.9 3.9 copy-start.2
  92.5 11.9 %copy-start.10 = (f32[8,512]{1,0:T(8,128)S(1)}, f32[8,512]{1,0:T(8,128)}, u32[]{:S(2)}) copy-start(f32[8,512]{1,0:T(8,128)} %param.11) | copy-start | bytes 49156
  94.4 99.6 %all-to-all-start = ((bf16[256,24,128]{2,1,0:T(8,128)(2,1)}), bf16[256,24,128]{2,1,0:T(8,128)(2,1)S(1)}, u32[]{:S(2)}, u32[]{:S(2)}) async-start(bf16[256,24,128]{2,1,0:T(8,128)(2,1)} %copy.75), calls=%async_computation | async-start | bytes 3145728 | tf_op jit(solution)/shard_map/all_to_all | solution.py:17
  204.1 4.5 copy-start.9
  208.6 1.4 copy-start.4
  210.0 1.7 copy-start.1
  211.7 1.7 copy-start.3
  232.4 52.8 %all-to-all-start.3 = ((bf16[256,24,128]{2,1,0:T(8,128)(2,1)}), bf16[256,24,128]{2,1,0:T(8,128)(2,1)}, u32[]{:S(2)}, u32[]{:S(2)}) async-start(bf16[256,24,128]{2,1,0:T(8,128)(2,1)} %reshape.161), calls=%async_computation.3 | async-start | bytes 3145728 | tf_op jit(solution)/shard_map/all_to_all | solution.py:17
  249.9 4.3 copy-start.8
  411.4 21.7 %all-to-all-start.7 = ((bf16[8,14,128]{2,1,0:T(8,128)(2,1)}), bf16[8,14,128]{2,1,0:T(8,128)(2,1)S(1)}, u32[]{:S(2)}, u32[]{:S(2)}) async-start(bf16[8,14,128]{2,1,0:T(8,128)(2,1)} %broadcast_in_dim.4), calls=%async_computation.7 | async-start | bytes 65536 | tf_op jit(solution)/shard_map/all_to_all | solution.py:17
  433.2 56.6 %all-to-all-start.1 = ((bf16[256,24,128]{2,1,0:T(8,128)(2,1)}), bf16[256,24,128]{2,1,0:T(8,128)(2,1)}, u32[]{:S(2)}, u32[]{:S(2)}) async-start(bf16[256,24,128]{2,1,0:T(8,128)(2,1)} %reshape.154), calls=%async_computation.1 | async-start | bytes 3145728 | tf_op jit(solution)/shard_map/all_to_all | solution.py:17
  491.0 36.9 %all-to-all-start.8 = ((bf16[32,152,128]{2,1,0:T(8,128)(2,1)}), bf16[32,152,128]{2,1,0:T(8,128)(2,1)S(1)}, u32[]{:S(2)}, u32[]{:S(2)}) async-start(bf16[32,152,128]{2,1,0:T(8,128)(2,1)} %broadcast_in_dim.5), calls=%async_computation.8 | async-start | bytes 2490368 | tf_op jit(solution)/shard_map/all_to_all | solution.py:17
  530.1 3.1 copy-start.6
Sparse Core Ops, SparseCore 0:
  19.5 64.4 all-gather.1

commit v2 on v1

v2 whole, which is shorter than its diff:
```python
import functools
import math

import jax
import jax.numpy as jnp
from jax import lax
from jax.experimental import pallas as pl
from jax.experimental.pallas import tpu as pltpu
from jax.sharding import Mesh
from jax.sharding import PartitionSpec as P

F32 = jnp.float32
BF16 = jnp.bfloat16
ALL = ("zh", "x", "y", "zl", "c")
DP = ("zh", "x")
CTX = ("y", "zl", "c")
LANES = 128
HALF = 64
NN = (((1,), (0,)), ((), ()))
NT = (((1,), (1,)), ((), ()))


def dot(a, b, dims=NN):
    return lax.dot_general(a, b, dims, preferred_element_type=F32)


def call(kernel, outs, scratch, flops, *args, smem=()):
    vmem = pl.BlockSpec(memory_space=pltpu.VMEM)
    specs = [pl.BlockSpec(memory_space=pltpu.SMEM) if i in smem else vmem for i in range(len(args))]
    moved = sum(a.size * a.dtype.itemsize for a in args)
    moved += sum(math.prod(s) * jnp.dtype(t).itemsize for s, t in outs)
    return pl.pallas_call(
        kernel,
        out_shape=[jax.ShapeDtypeStruct(s, t) for s, t in outs],
        in_specs=specs,
        out_specs=[vmem] * len(outs),
        scratch_shapes=scratch,
        compiler_params=pltpu.CompilerParams(vmem_limit_bytes=56 * 2**20),
        cost_estimate=pl.CostEstimate(flops=flops, bytes_accessed=moved, transcendentals=0),
    )(*args)


def widen(lines_ref, buf):
    for r in range(0, buf.shape[0], 512):
        buf[r : r + 512, :] = lines_ref[r : r + 512, :].astype(F32)


def narrow(buf, lines_ref):
    for r in range(0, buf.shape[0], 512):
        lines_ref[r : r + 512, :] = buf[r : r + 512, :].astype(BF16)


def home_store(buf, j, value, count, groups):
    for g in range(groups):
        buf[pl.ds(j * groups + g, value.shape[0], stride=count), :] = value[:, g * LANES : (g + 1) * LANES]


def home_load(buf, j, out_ref, devices, count, groups):
    for g in range(groups):
        value = buf[pl.ds(j * groups + g, devices, stride=count), :]
        out_ref[j * devices : (j + 1) * devices, g * LANES : (g + 1) * LANES] = value.astype(BF16)


def chan_load(buf, j, out_ref, count, groups):
    low = lax.broadcasted_iota(jnp.int32, (32, LANES), 1) < HALF
    for g in range(groups):
        for p in range(4):
            a = buf[pl.ds(2 * p * 32 * count + j * groups + g, 32, stride=count), :]
            b = buf[pl.ds((2 * p + 1) * 32 * count + j * groups + g, 32, stride=count), :]
            even = jnp.where(low, a, pltpu.roll(b, HALF, 1))
            odd = jnp.where(low, pltpu.roll(a, HALF, 1), b)
            lanes = slice(p * LANES, (p + 1) * LANES)
            out_ref[j, 2 * g * 32 : (2 * g + 1) * 32, lanes] = even.astype(BF16)
            out_ref[j, (2 * g + 1) * 32 : (2 * g + 2) * 32, lanes] = odd.astype(BF16)


def chan_store(buf, j, value, count, groups):
    low = lax.broadcasted_iota(jnp.int32, (32, LANES), 1) < HALF
    for g in range(groups):
        for p in range(4):
            lanes = slice(p * LANES, (p + 1) * LANES)
            even = value[2 * g * 32 : (2 * g + 1) * 32, lanes]
            odd = value[(2 * g + 1) * 32 : (2 * g + 2) * 32, lanes]
            a = jnp.where(low, even, pltpu.roll(odd, HALF, 1))
            b = jnp.where(low, pltpu.roll(even, HALF, 1), odd)
            buf[pl.ds(2 * p * 32 * count + j * groups + g, 32, stride=count), :] = a
            buf[pl.ds((2 * p + 1) * 32 * count + j * groups + g, 32, stride=count), :] = b


def unit(size):
    rows = lax.broadcasted_iota(jnp.int32, (size, size), 0)
    cols = lax.broadcasted_iota(jnp.int32, (size, size), 1)
    return jnp.where(rows == cols, 1.0, 0.0).astype(BF16)


def pack_x(count, groups, x_ref, out_ref, buf):
    devices = out_ref.shape[0] // count
    eye = unit(devices)
    for j in range(count // groups):
        turned = dot(eye, x_ref[:, j * devices : (j + 1) * devices], NT)
        home_store(buf, j, turned, count, groups)
    narrow(buf, out_ref)


def pack_h(count, groups, x_ref, cot_ref, w_ref, out_ref, grad_ref, buf):
    devices = out_ref.shape[0] // count
    grad = (cot_ref[...].astype(F32) * x_ref[...].astype(F32)).astype(BF16)
    grad_ref[...] = grad
    for j in range(count // groups):
        value = dot(w_ref[j * devices : (j + 1) * devices, :], grad_ref[...], NT)
        home_store(buf, j, value, count, groups)
    narrow(buf, out_ref)


def forward(count, groups, got_ref, one_ref, two_ref, scale_ref, out_ref, x_ref, y_ref, s_ref, buf, back):
    widen(got_ref, buf)
    for j in range(count // groups):
        chan_load(buf, j, x_ref, count, groups)
        y = dot(x_ref[j], one_ref[...], NT)
        y_ref[j] = y
        s_ref[j] = (scale_ref[...] * y).astype(BF16)
        chan_store(back, j, dot(two_ref[...], s_ref[j]), count, groups)
    narrow(back, out_ref)


def backward(count, groups, got_ref, one_ref, two_ref, scale_ref, y_ref, out_ref, h_ref, t_ref, term_ref, buf, back):
    widen(got_ref, buf)
    for j in range(count // groups):
        chan_load(buf, j, h_ref, count, groups)
        u = dot(two_ref[...], h_ref[j])
        if j == 0:
            term_ref[...] = u * y_ref[j]
        else:
            term_ref[...] += u * y_ref[j]
        t_ref[j] = (scale_ref[...] * u).astype(BF16)
        chan_store(back, j, dot(t_ref[j], one_ref[...]), count, groups)
    narrow(back, out_ref)


def win_parts(count, groups, core_ref, got_ref, grad_ref, mixed_ref, mine_ref, other_ref, buf):
    devices = got_ref.shape[0] // count
    widen(got_ref, buf)
    for j in range(count // groups):
        home_load(buf, j, mixed_ref, devices, count, groups)
    half = mixed_ref.shape[0] // 16
    core = core_ref[0]
    for d in range(8):
        rows = slice(d * half, (d + 1) * half)
        far = pl.multiple_of(d * 2 * half + (1 - core) * half, 32)
        near = pl.multiple_of(d * 2 * half + core * half, 32)
        other_ref[rows, :] = dot(mixed_ref[pl.ds(far, half), :], grad_ref[...]).astype(BF16)
        mine_ref[rows, :] = dot(mixed_ref[pl.ds(near, half), :], grad_ref[...]).astype(BF16)


def mix(mixed_ref, w_ref, out_ref, flat):
    flat[...] = dot(unit(mixed_ref.shape[1]), mixed_ref[...], NT).astype(BF16)
    out_ref[...] = dot(flat[...], w_ref[...]).astype(BF16)


def finish(count, groups, got_ref, cot_ref, mixed_ref, out_ref, buf, turned):
    devices = got_ref.shape[0] // count
    widen(got_ref, buf)
    eye = unit(turned.shape[1])
    for j in range(count // groups):
        home_load(buf, j, turned, devices, count, groups)
        cols = slice(j * devices, (j + 1) * devices)
        back = dot(eye, turned[cols, :], NT)
        gate = cot_ref[:, cols].astype(F32) * mixed_ref[:, cols].astype(F32)
        out_ref[:, cols] = (back + gate).astype(BF16)


def shifted(array, axis, size, step):
    return lax.ppermute(array, axis, [(i, (i + step) % size) for i in range(size)])


def sum_scatter(parts, axis, size):
    me = lax.axis_index(axis)
    total = lax.dynamic_index_in_dim(parts, me, 0, False).astype(F32)
    for step in range(1, size):
        part = lax.dynamic_index_in_dim(parts, (me + step) % size, 0, False)
        total = total + shifted(part, axis, size, step).astype(F32)
    return total


def sum_all(part, axis, size):
    total = part.astype(F32)
    for step in range(1, size):
        total = total + shifted(part, axis, size, step).astype(F32)
    return total


def gather(piece, axis, size):
    me = lax.axis_index(axis)
    pieces = [piece] + [shifted(piece, axis, size, step) for step in range(1, size)]
    held = jnp.stack(pieces)
    return jnp.stack([lax.dynamic_index_in_dim(held, (me - i) % size, 0, False) for i in range(size)])


def gather_w(w_in):
    rows, width = w_in.shape
    piece = rows // 8
    place = lax.axis_index("y") * 2 + lax.axis_index("c")
    mine = lax.dynamic_slice_in_dim(w_in, place * piece, piece, 0)
    other = lax.ppermute(mine, "zh", [(0, 1), (1, 0)])
    low = lax.axis_index("zh") == 0
    both = jnp.concatenate([jnp.where(low, mine, other), jnp.where(low, other, mine)], 0)
    whole = lax.all_gather(both, ("x", "y", "c"), axis=0, tiled=True)
    whole = whole.reshape(4, 8, 2, piece, width).transpose(2, 0, 1, 3, 4)
    return whole.reshape(8 * rows, width)


def exchange(lines):
    return lax.all_to_all(lines, ALL, 0, 0, tiled=True)


def per_device(inputs, cotangent, w_in, factor_one, factor_two, kernel):
    blocks, pos, width = inputs.shape
    tokens = blocks * pos
    devices = 256
    chans = width // devices
    groups = tokens // LANES
    count = chans * groups
    block_len = factor_one.shape[0]
    block_count = factor_two.shape[0]
    lines = (devices * count, LANES)
    buf = pltpu.VMEM(lines, F32)
    shape = (chans, block_count, block_len)
    work = 2 * chans * block_count * block_len
    square = 2 * tokens * width * width

    rows_in = inputs.reshape(tokens, width)
    cot_rows = cotangent.reshape(tokens, width)
    (x_lines,) = call(
        functools.partial(pack_x, count, groups), [(lines, BF16)], [buf], 2 * tokens * width * devices, rows_in
    )
    scale = gather(gather(gather(kernel, "c", 2), "zl", 4), "y", 4)
    scale = scale.reshape(block_count // blocks, blocks, block_len).transpose(1, 0, 2)
    scale = scale.reshape(block_count, block_len)
    two = factor_two.reshape(32, 8, 32, 8).transpose(1, 0, 3, 2).reshape(block_count, block_count)
    whole_w = gather_w(w_in)

    x_got = exchange(x_lines)
    m_lines, xc, yc, sc = call(
        functools.partial(forward, count, groups),
        [(lines, BF16), (shape, BF16), (shape, F32), (shape, BF16)],
        [buf, buf],
        work * (block_len + block_count),
        x_got,
        factor_one,
        two,
        scale,
    )
    m_got = exchange(m_lines)
    h_lines, grad_mixed = call(
        functools.partial(pack_h, count, groups),
        [(lines, BF16), ((tokens, width), BF16)],
        [buf],
        square,
        rows_in,
        cot_rows,
        whole_w,
    )
    h_lines, m_got = lax.optimization_barrier((h_lines, m_got))
    h_got = exchange(h_lines)
    core = lax.axis_index("c")
    mixed_t, mine, other = call(
        functools.partial(win_parts, count, groups),
        [((width, tokens), BF16), ((width // 2, width), BF16), ((width // 2, width), BF16)],
        [buf],
        square,
        core.astype(jnp.int32).reshape(1),
        m_got,
        grad_mixed,
        smem=(0,),
    )
    (mixed,) = call(
        mix, [((tokens, width), BF16)], [pltpu.VMEM((tokens, width), BF16)], square, mixed_t, whole_w
    )
    win = mine.astype(F32) + shifted(other, "c", 2, 1).astype(F32)
    win = win.astype(BF16).reshape(2, 4, 4, -1, width)
    win = sum_scatter(win.transpose(2, 0, 1, 3, 4), "y", 4).astype(BF16)
    win = sum_scatter(win.transpose(1, 0, 2, 3), "x", 4).astype(BF16)
    win = sum_scatter(win, "zh", 2).astype(BF16)
    win = sum_all(win, "zl", 4).astype(BF16)
    win = gather(gather(win, "y", 4), "c", 2).reshape(width // 8, width)
    grad_w_in = win.astype(F32) / math.sqrt(block_count * block_len)

    b_lines, hc, tc, kernel_term = call(
        functools.partial(backward, count, groups),
        [(lines, BF16), (shape, BF16), (shape, BF16), (shape[1:], F32)],
        [buf, buf],
        work * (block_len + block_count),
        h_got,
        factor_one,
        two.T,
        scale,
        yc,
    )
    b_got = exchange(b_lines)
    one_term = jnp.einsum("jap,jaq->pq", tc, xc, preferred_element_type=F32)
    two_term = jnp.einsum("jip,jlp->il", hc, sc, preferred_element_type=F32)
    sizes = (one_term.size // LANES, two_term.size // LANES, kernel_term.size // LANES)
    small = jnp.concatenate([a.reshape(-1, LANES).astype(BF16) for a in (one_term, two_term, kernel_term)], 0)
    small = sum_scatter(small.reshape(2, -1, LANES), "c", 2).astype(BF16)
    small = sum_scatter(small.reshape(4, -1, LANES), "y", 4).astype(BF16)
    small = sum_scatter(small.reshape(4, -1, LANES), "x", 4).astype(BF16)
    small = sum_all(small, "zh", 2).astype(BF16)
    small = sum_all(small, "zl", 4).astype(BF16)
    small = gather(gather(gather(small, "x", 4), "y", 4), "c", 2).reshape(-1, LANES)
    one_total = small[: sizes[0]].astype(F32).reshape(block_len, block_len)
    two_total = small[sizes[0] : sizes[0] + sizes[1]].astype(F32)
    two_total = two_total.reshape(8, 32, 8, 32).transpose(1, 0, 3, 2).reshape(block_count, block_count)
    kernel_total = small[sizes[0] + sizes[1] :].reshape(8, 32, block_len)
    place = (lax.axis_index("y") * 4 + lax.axis_index("zl")) * 2 + core
    kernel_total = lax.dynamic_index_in_dim(kernel_total, place, 1, False).astype(F32)
    grad_kernel = kernel_total / math.sqrt(width)
    grad_one = one_total / math.sqrt(block_count * width)
    grad_two = two_total / math.sqrt(block_len * width)

    (grad_in,) = call(
        functools.partial(finish, count, groups),
        [((tokens, width), BF16)],
        [buf, pltpu.VMEM((width, tokens), BF16)],
        2 * tokens * tokens * width,
        b_got,
        cot_rows,
        mixed,
    )
    return (grad_in.reshape(inputs.shape), grad_w_in, grad_one, grad_two, grad_kernel)


def solution(mesh):
    fine = Mesh(mesh.devices.reshape(2, 4, 4, 4, 2), ALL)
    return jax.shard_map(
        per_device,
        mesh=fine,
        in_specs=(
            P(CTX, DP, None),
            P(CTX, DP, None),
            P(DP, None),
            P(),
            P(),
            P(CTX, None),
        ),
        out_specs=(P(CTX, DP, None), P(DP, None), P(), P(), P(CTX, None)),
        check_vma=False,
    )
```

time: 550 us -> 359 us (0.65)
  blocking collectives: 132 us -> 0 us
  local copies, waits for them, and re-layouts: 151 us -> 30.6 us
  starting transfers between devices: 68.9 us -> 122 us
  Pallas kernels: 0 us -> 47.3 us
  matrix products: 31.4 us -> 4.95 us
  other arithmetic: 17.5 us -> 9.62 us
    ppermute x0 -> x40, waiting for transfers between devices: none -> 91.3 us  [shifted(): lax.ppermute(array, axis, [(i, (i + step) % size) for i in range(size)])]
    all_gather x1 -> x0, blocking collectives: 71.5 us -> none  [per_device(): scale = lax.all_gather(kernel, CTX, axis=0, tiled=True)]
    ppermute x0 -> x40, starting transfers between devices: none -> 71.4 us  [shifted(): lax.ppermute(array, axis, [(i, (i + step) % size) for i in range(size)])]
    reshape x18 -> x6, local copies, waits for them, and re-layouts: 70.5 us -> 9.83 us  [the longest x1 4.99 us: gather_w(): whole = whole.reshape(4, 8, 2, piece, width).transpose(2, 0, 1, 3, 4)]
    all_to_all x3 -> x0, blocking collectives: 60 us -> none  [exchange(): return lax.all_to_all(array, axes, 0, 0, tiled=True)]
    all_to_all x6 -> x4, waiting for transfers between devices: 85.5 us -> 29.8 us  [exchange(): return lax.all_to_all(lines, ALL, 0, 0, tiled=True)]
    pallas_call x0 -> x7, Pallas kernels: none -> 47.3 us  [call(): pl.pallas_call(kernel, out_shape=[jax.ShapeDtypeStruct(s, t) for s, t in...]
    all_gather x1, waiting for transfers between devices: 39.1 us -> 0.02 us  [gather_w(): whole = lax.all_gather(both, ('x', 'y', 'c'), axis=0, tiled=True)]
  transfers between devices with their start and end apart: 8 -> 46, of which waited for: 5 -> 19; matrix products, arithmetic and copies ran while one was open for 16% -> 11% of each run, Pallas kernels for 0% -> 9%
where the time goes in v2:
time: 359 us; the launch traced here: 353 us
  waiting for transfers between devices  123 us (34%)
  starting transfers between devices  122 us (34%)
  Pallas kernels  47.3 us (13%)
  local copies, waits for them, and re-layouts  30.6 us (9%)
  between operations  15 us (4%)
  other arithmetic  9.62 us (3%)
  matrix products  4.95 us (1%)
    ppermute x40, waiting for transfers between devices, shifted(): lax.ppermute(array, axis, [(i, (i + step) % size) for i in range(size)])  91.3 us
    ppermute x40, starting transfers between devices, shifted(): lax.ppermute(array, axis, [(i, (i + step) % size) for i in range(size)])  71.4 us
    pallas_call x7, Pallas kernels, call(): pl.pallas_call(kernel, out_shape=[jax.ShapeDtypeStruct(s, t) for s, t in...  47.3 us
    all_to_all x4, starting transfers between devices, exchange(): return lax.all_to_all(lines, ALL, 0, 0, tiled=True)  43.1 us
    all_to_all x4, waiting for transfers between devices, exchange(): return lax.all_to_all(lines, ALL, 0, 0, tiled=True)  29.8 us
    div x3, local copies, waits for them, and re-layouts, per_device(): grad_two = two_total / math.sqrt(block_len * width)  8.63 us
    ppermute x1, starting transfers between devices, gather_w(): other = lax.ppermute(mine, 'zh', [(0, 1), (1, 0)])  7.74 us
  transfers between devices with their start and end apart: 46, of which 19 were waited for; matrix products, arithmetic and copies ran while one was open for 11% of the time, Pallas kernels for 9%

profile of v2, /device:TPU:1, one launch (start us, length us, event | category | flops | bytes accessed | tf_op | source)
XLA Modules:
  0.0 352.9 jit_solution(9341089976302618610)
XLA Ops:
  8.1 7.7 %collective-permute-start = (bf16[24,1536]{1,0:T(8,128)(2,1)S(1)}, bf16[24,1536]{1,0:T(8,128)(2,1)S(1)}, u32[]{:S(2)}, u32[]{:S(2)}) collective-permute-start(bf16[24,1536]{1,0:T(8,128)(2,1)S(1)} %constant_dynamic-slice_fusion.20), channel_id=1, source_target_pairs={{0,128},{128,0},{1,129},{129,1},{2,130},{130,2},{3,131},{131,3},{4... | collective-permute-start | bytes 221192 | tf_op jit(solution)/shard_map/ppermute | solution.py:204
  19.3 3.5 shard_map.102
  22.8 16.3 %all-to-all-start = ((bf16[256,24,128]{2,1,0:T(8,128)(2,1)}), bf16[256,24,128]{2,1,0:T(8,128)(2,1)}, u32[]{:S(2)}, u32[]{:S(2)}) async-start(bf16[256,24,128]{2,1,0:T(8,128)(2,1)} %bitcast.130), calls=%async_computation | async-start | bytes 3145728 | tf_op jit(solution)/shard_map/all_to_all | solution.py:213
  45.7 27.7 %collective-permute-done.2 = f32[2,8,512]{2,1,0:T(8,128)S(1)} collective-permute-done((f32[2,8,512]{2,1,0:T(8,128)S(1)}, f32[2,8,512]{2,1,0:T(8,128)S(1)}, u32[]{:S(2)}, u32[]{:S(2)}) %collective-permute-start.2) | collective-permute-done | bytes 32800 | tf_op jit(solution)/shard_map/ppermute | solution.py:173
  87.2 7.6 %shard_map.103 = (bf16[6144,128]{1,0:T(8,128)(2,1)}, bf16[6,256,512]{2,1,0:T(8,128)(2,1)}, f32[6,256,512]{2,1,0:T(8,128)}, bf16[6,256,512]{2,1,0:T(8,128)(2,1)}) custom-call(bf16[6144,128]{1,0:T(8,128)(2,1)} %bitcast.6.got_ref, bf16[512,512]{1,0:T(8,128)(2,1)} %one_ref.3, bf16[256,256]{1,0:T(8,128)(2,1)} %copy.19.two_ref, f32[256,512]{1,0:T(8,128)} %bitcast.141), custom_call_target="tpu_custom_call" | custom-call | flops 1207959552 | bytes 10616832 | tf_op jit(solution)/shard_map/pallas_call | solution.py:32
  94.7 12.8 %all-to-all-start.1 = ((bf16[256,24,128]{2,1,0:T(8,128)(2,1)}), bf16[256,24,128]{2,1,0:T(8,128)(2,1)S(1)}, u32[]{:S(2)}, u32[]{:S(2)}) async-start(bf16[256,24,128]{2,1,0:T(8,128)(2,1)} %bitcast.151), calls=%async_computation.1 | async-start | bytes 3145728 | tf_op jit(solution)/shard_map/all_to_all | solution.py:213
  107.6 5.0 %copy.16 = bf16[4,8,2,24,1536]{4,3,1,0,2:T(8,128)(2,1)} copy(bf16[4,8,2,24,1536]{4,3,2,1,0:T(8,128)(2,1)} %bitcast.134) | data formatting | bytes 9437184 | tf_op jit(solution)/shard_map/reshape | solution.py:208
  112.6 7.3 %shard_map.101 = (bf16[6144,128]{1,0:T(8,128)(2,1)}, bf16[512,1536]{1,0:T(8,128)(2,1)}) custom-call(bf16[512,1536]{1,0:T(8,128)(2,1)} %bitcast.147, bf16[512,1536]{1,0:T(8,128)(2,1)} %bitcast.152, bf16[1536,1536]{1,0:T(8,128)(2,1)} %bitcast.132), custom_call_target="tpu_custom_call" | custom-call | flops 2415919104 | bytes 11010048 | tf_op jit(solution)/shard_map/pallas_call | solution.py:32
  119.9 29.8 %all-to-all-done.1 = bf16[256,24,128]{2,1,0:T(8,128)(2,1)S(1)} async-done(((bf16[256,24,128]{2,1,0:T(8,128)(2,1)}), bf16[256,24,128]{2,1,0:T(8,128)(2,1)S(1)}, u32[]{:S(2)}, u32[]{:S(2)}) %all-to-all-start.1) | async-done | bytes 1572896 | tf_op jit(solution)/shard_map/all_to_all | solution.py:213
  150.9 9.0 %shard_map.105 = (bf16[1536,512]{1,0:T(8,128)(2,1)}, bf16[768,1536]{1,0:T(8,128)(2,1)}, bf16[768,1536]{1,0:T(8,128)(2,1)}) custom-call(s32[1]{0:T(128)} %bitcast.28.core_ref, bf16[6144,128]{1,0:T(8,128)(2,1)} %bitcast.150, bf16[512,1536]{1,0:T(8,128)(2,1)} %get-tuple-element.26.grad_ref), custom_call_target="tpu_custom_call" | custom-call | flops 2415919104 | bytes 9437188 | tf_op jit(solution)/shard_map/pallas_call | solution.py:32
  159.8 7.4 %all-to-all-start.2 = ((bf16[256,24,128]{2,1,0:T(8,128)(2,1)}), bf16[256,24,128]{2,1,0:T(8,128)(2,1)}, u32[]{:S(2)}, u32[]{:S(2)}) async-start(bf16[256,24,128]{2,1,0:T(8,128)(2,1)} %bitcast.148), calls=%async_computation.2 | async-start | bytes 3145728 | tf_op jit(solution)/shard_map/all_to_all | solution.py:213
  177.4 7.4 %shard_map.106.mixed_ref = bf16[512,1536]{1,0:T(8,128)(2,1)} custom-call(bf16[1536,512]{1,0:T(8,128)(2,1)} %get-tuple-element.27.mixed_ref, bf16[1536,1536]{1,0:T(8,128)(2,1)} %bitcast.133), custom_call_target="tpu_custom_call" | custom-call | flops 2415919104 | bytes 7864320 | tf_op jit(solution)/shard_map/pallas_call | solution.py:32
  184.9 13.7 %collective-permute-done.10 = bf16[2,4,24,1536]{3,2,1,0:T(8,128)(2,1)S(1)} collective-permute-done((bf16[2,4,24,1536]{3,2,1,0:T(8,128)(2,1)}, bf16[2,4,24,1536]{3,2,1,0:T(8,128)(2,1)S(1)}, u32[]{:S(2)}, u32[]{:S(2)}) %collective-permute-start.10) | collective-permute-done | bytes 589856 | tf_op jit(solution)/shard_map/ppermute | solution.py:173
  198.6 17.0 %collective-permute-done.11 = bf16[2,4,24,1536]{3,2,1,0:T(8,128)(2,1)} collective-permute-done((bf16[2,4,24,1536]{3,2,1,0:T(8,128)(2,1)}, bf16[2,4,24,1536]{3,2,1,0:T(8,128)(2,1)}, u32[]{:S(2)}, u32[]{:S(2)}) %collective-permute-start.11) | collective-permute-done | bytes 589856 | tf_op jit(solution)/shard_map/ppermute | solution.py:173
  221.7 7.5 %shard_map.104 = (bf16[6144,128]{1,0:T(8,128)(2,1)}, bf16[6,256,512]{2,1,0:T(8,128)(2,1)}, bf16[6,256,512]{2,1,0:T(8,128)(2,1)}, f32[256,512]{1,0:T(8,128)}) custom-call(bf16[6144,128]{1,0:T(8,128)(2,1)} %bitcast.24.got_ref, bf16[512,512]{1,0:T(8,128)(2,1)} %one_ref.3, bf16[256,256]{1,0:T(8,128)(2,1)} %bitcast.155, f32[256,512]{1,0:T(8,128)} %bitcast.142, ...), custom_call_target="tpu_custom_call" | custom-call | flops 1207959552 | bytes 11141120 | tf_op jit(solution)/shard_map/pallas_call | solution.py:32
  241.7 4.8 %collective-permute-start.15 = (bf16[24,1536]{1,0:T(8,128)(2,1)S(1)}, bf16[24,1536]{1,0:T(8,128)(2,1)S(1)}, u32[]{:S(2)}, u32[]{:S(2)}) collective-permute-start(bf16[24,1536]{1,0:T(8,128)(2,1)S(1)} %dynamic-slice_bitcast_fusion.10), channel_id=1, source_target_pairs={{0,128},{128,0},{1,129},{129,1},{2,130},{130,2},{3,131},{131,3},{4... | collective-permute-start | bytes 221192 | tf_op jit(solution)/shard_map/ppermute | solution.py:173
  246.5 6.6 %all-to-all-start.3 = ((bf16[256,24,128]{2,1,0:T(8,128)(2,1)}), bf16[256,24,128]{2,1,0:T(8,128)(2,1)S(1)}, u32[]{:S(2)}, u32[]{:S(2)}) async-start(bf16[256,24,128]{2,1,0:T(8,128)(2,1)} %bitcast.149), calls=%async_computation.3 | async-start | bytes 3145728 | tf_op jit(solution)/shard_map/all_to_all | solution.py:213
  263.4 4.9 %collective-permute-start.30 = (bf16[112,128]{1,0:T(8,128)(2,1)S(1)}, bf16[112,128]{1,0:T(8,128)(2,1)S(1)}, u32[]{:S(2)}, u32[]{:S(2)}) collective-permute-start(bf16[112,128]{1,0:T(8,128)(2,1)S(1)} %fusion.19), channel_id=1, source_target_pairs={{0,128},{128,0},{1,129},{129,1},{2,130},{130,2},{3,131},{131,3},{4... | collective-permute-start | bytes 86024 | tf_op jit(solution)/shard_map/ppermute | solution.py:173
  268.2 21.5 %collective-permute-done.16 = bf16[24,1536]{1,0:T(8,128)(2,1)S(1)} collective-permute-done((bf16[24,1536]{1,0:T(8,128)(2,1)S(1)}, bf16[24,1536]{1,0:T(8,128)(2,1)S(1)}, u32[]{:S(2)}, u32[]{:S(2)}) %collective-permute-start.16) | collective-permute-done | bytes 73760 | tf_op jit(solution)/shard_map/ppermute | solution.py:173
  289.7 3.4 collective-permute-done.17
  315.8 4.8 %collective-permute-start.22 = (bf16[4,24,1536]{2,1,0:T(8,128)(2,1)S(1)}, bf16[4,24,1536]{2,1,0:T(8,128)(2,1)S(1)}, u32[]{:S(2)}, u32[]{:S(2)}) collective-permute-start(bf16[4,24,1536]{2,1,0:T(8,128)(2,1)S(1)} %get-tuple-element.58), channel_id=1, source_target_pairs={{0,1},{1,0},{2,3},{3,2},{4,5},{5,4},{6,7},{7,6},{8,9},{9,8},{10,11... | collective-permute-start | bytes 884744 | tf_op jit(solution)/shard_map/ppermute | solution.py:173
  320.8 4.7 %collective-permute-start.40 = (bf16[4,4,112,128]{3,2,1,0:T(8,128)(2,1)S(1)}, bf16[4,4,112,128]{3,2,1,0:T(8,128)(2,1)S(1)}, u32[]{:S(2)}, u32[]{:S(2)}) collective-permute-start(bf16[4,4,112,128]{3,2,1,0:T(8,128)(2,1)S(1)} %get-tuple-element.49), channel_id=1, source_target_pairs={{0,1},{1,0},{2,3},{3,2},{4,5},{5,4},{6,7},{7,6},{8,9},{9,8},{10,11... | collective-permute-start | bytes 1376264 | tf_op jit(solution)/shard_map/ppermute | solution.py:173
  332.7 4.7 %div.46 = f32[256,256]{1,0:T(8,128)} reshape(f32[32,8,32,8]{3,2,1,0:T(8,128)} %copy.21) | data formatting | bytes 524288 | tf_op jit(solution)/shard_map/div | solution.py:318
  340.6 5.0 %shard_map.107 = bf16[512,1536]{1,0:T(8,128)(2,1)} custom-call(bf16[6144,128]{1,0:T(8,128)(2,1)} %bitcast.131, bf16[512,1536]{1,0:T(8,128)(2,1)} %bitcast.153, bf16[512,1536]{1,0:T(8,128)(2,1)} %shard_map.106.mixed_ref), custom_call_target="tpu_custom_call" | custom-call | flops 805306368 | bytes 6291456 | tf_op jit(solution)/shard_map/pallas_call | solution.py:32
  (157 shorter events, 97.9 us)
Async XLA Ops:
  7.2 100.4 %all-gather.2.cloned.1.call-start = ((), (), s32[]{:S(2)}) async-start(), calls=%async_computation.4 | async-start | bytes 4866048 | tf_op jit(solution)/shard_map/all_gather | solution.py:207
  22.8 64.3 %all-to-all-start = ((bf16[256,24,128]{2,1,0:T(8,128)(2,1)}), bf16[256,24,128]{2,1,0:T(8,128)(2,1)}, u32[]{:S(2)}, u32[]{:S(2)}) async-start(bf16[256,24,128]{2,1,0:T(8,128)(2,1)} %bitcast.130), calls=%async_computation | async-start | bytes 3145728 | tf_op jit(solution)/shard_map/all_to_all | solution.py:213
  42.3 31.0 %collective-permute-start.2 = (f32[2,8,512]{2,1,0:T(8,128)S(1)}, f32[2,8,512]{2,1,0:T(8,128)S(1)}, u32[]{:S(2)}, u32[]{:S(2)}) collective-permute-start(f32[2,8,512]{2,1,0:T(8,128)S(1)} %get-tuple-element.82), channel_id=1, source_target_pairs={{0,2},{2,4},{4,6},{6,0},{1,3},{3,5},{5,7},{7,1},{8,10},{10,12},{12... | collective-permute-start | bytes 98312 | tf_op jit(solution)/shard_map/ppermute | solution.py:173
  42.4 31.5 %collective-permute-start.3 = (f32[2,8,512]{2,1,0:T(8,128)S(1)}, f32[2,8,512]{2,1,0:T(8,128)S(1)}, u32[]{:S(2)}, u32[]{:S(2)}) collective-permute-start(f32[2,8,512]{2,1,0:T(8,128)S(1)} %get-tuple-element.82), channel_id=1, source_target_pairs={{0,4},{2,6},{4,0},{6,2},{1,5},{3,7},{5,1},{7,3},{8,12},{10,14},{12... | collective-permute-start | bytes 98312 | tf_op jit(solution)/shard_map/ppermute | solution.py:173
  44.7 29.4 %collective-permute-start.4 = (f32[2,8,512]{2,1,0:T(8,128)S(1)}, f32[2,8,512]{2,1,0:T(8,128)S(1)}, u32[]{:S(2)}, u32[]{:S(2)}) collective-permute-start(f32[2,8,512]{2,1,0:T(8,128)S(1)} %get-tuple-element.82), channel_id=1, source_target_pairs={{0,6},{2,0},{4,2},{6,4},{1,7},{3,1},{5,3},{7,5},{8,14},{10,8},{12,... | collective-permute-start | bytes 98312 | tf_op jit(solution)/shard_map/ppermute | solution.py:173
  74.2 11.7 %collective-permute-start.5 = (f32[4,2,8,512]{3,2,1,0:T(8,128)S(1)}, f32[4,2,8,512]{3,2,1,0:T(8,128)S(1)}, u32[]{:S(2)}, u32[]{:S(2)}) collective-permute-start(f32[4,2,8,512]{3,2,1,0:T(8,128)S(1)} %get-tuple-element.67), channel_id=1, source_target_pairs={{0,8},{8,16},{16,24},{24,0},{1,9},{9,17},{17,25},{25,1},{2,10},{10... | collective-permute-start | bytes 393224 | tf_op jit(solution)/shard_map/ppermute | solution.py:173
  75.5 10.4 %collective-permute-start.6 = (f32[4,2,8,512]{3,2,1,0:T(8,128)S(1)}, f32[4,2,8,512]{3,2,1,0:T(8,128)S(1)}, u32[]{:S(2)}, u32[]{:S(2)}) collective-permute-start(f32[4,2,8,512]{3,2,1,0:T(8,128)S(1)} %get-tuple-element.67), channel_id=1, source_target_pairs={{0,16},{8,24},{16,0},{24,8},{1,17},{9,25},{17,1},{25,9},{2,18},{10... | collective-permute-start | bytes 393224 | tf_op jit(solution)/shard_map/ppermute | solution.py:173
  94.7 55.0 %all-to-all-start.1 = ((bf16[256,24,128]{2,1,0:T(8,128)(2,1)}), bf16[256,24,128]{2,1,0:T(8,128)(2,1)S(1)}, u32[]{:S(2)}, u32[]{:S(2)}) async-start(bf16[256,24,128]{2,1,0:T(8,128)(2,1)} %bitcast.151), calls=%async_computation.1 | async-start | bytes 3145728 | tf_op jit(solution)/shard_map/all_to_all | solution.py:213
  159.8 61.8 %all-to-all-start.2 = ((bf16[256,24,128]{2,1,0:T(8,128)(2,1)}), bf16[256,24,128]{2,1,0:T(8,128)(2,1)}, u32[]{:S(2)}, u32[]{:S(2)}) async-start(bf16[256,24,128]{2,1,0:T(8,128)(2,1)} %bitcast.148), calls=%async_computation.2 | async-start | bytes 3145728 | tf_op jit(solution)/shard_map/all_to_all | solution.py:213
  173.0 25.6 %collective-permute-start.10 = (bf16[2,4,24,1536]{3,2,1,0:T(8,128)(2,1)}, bf16[2,4,24,1536]{3,2,1,0:T(8,128)(2,1)S(1)}, u32[]{:S(2)}, u32[]{:S(2)}) collective-permute-start(bf16[2,4,24,1536]{3,2,1,0:T(8,128)(2,1)} %get-tuple-element.37), channel_id=1, source_target_pairs={{0,16},{8,24},{16,0},{24,8},{1,17},{9,25},{17,1},{25,9},{2,18},{10... | collective-permute-start | bytes 1769480 | tf_op jit(solution)/shard_map/ppermute | solution.py:173
  175.8 39.8 %collective-permute-start.11 = (bf16[2,4,24,1536]{3,2,1,0:T(8,128)(2,1)}, bf16[2,4,24,1536]{3,2,1,0:T(8,128)(2,1)}, u32[]{:S(2)}, u32[]{:S(2)}) collective-permute-start(bf16[2,4,24,1536]{3,2,1,0:T(8,128)(2,1)} %get-tuple-element.36), channel_id=1, source_target_pairs={{0,24},{8,0},{16,8},{24,16},{1,25},{9,1},{17,9},{25,17},{2,26},{10... | collective-permute-start | bytes 1769480 | tf_op jit(solution)/shard_map/ppermute | solution.py:173
  176.7 39.1 %collective-permute-start.9 = (bf16[2,4,24,1536]{3,2,1,0:T(8,128)(2,1)S(1)}, bf16[2,4,24,1536]{3,2,1,0:T(8,128)(2,1)}, u32[]{:S(2)}, u32[]{:S(2)}) collective-permute-start(bf16[2,4,24,1536]{3,2,1,0:T(8,128)(2,1)S(1)} %get-tuple-element.35), channel_id=1, source_target_pairs={{0,8},{8,16},{16,24},{24,0},{1,9},{9,17},{17,25},{25,1},{2,10},{10... | collective-permute-start | bytes 1769480 | tf_op jit(solution)/shard_map/ppermute | solution.py:173
  217.5 18.9 %collective-permute-start.12 = (bf16[2,24,1536]{2,1,0:T(8,128)(2,1)S(1)}, bf16[2,24,1536]{2,1,0:T(8,128)(2,1)S(1)}, u32[]{:S(2)}, u32[]{:S(2)}) collective-permute-start(bf16[2,24,1536]{2,1,0:T(8,128)(2,1)S(1)} %get-tuple-element.42), channel_id=1, source_target_pairs={{0,32},{32,64},{64,96},{96,0},{1,33},{33,65},{65,97},{97,1},{2,34}... | collective-permute-start | bytes 442376 | tf_op jit(solution)/shard_map/ppermute | solution.py:173
  218.3 18.1 %collective-permute-start.13 = (bf16[2,24,1536]{2,1,0:T(8,128)(2,1)S(1)}, bf16[2,24,1536]{2,1,0:T(8,128)(2,1)S(1)}, u32[]{:S(2)}, u32[]{:S(2)}) collective-permute-start(bf16[2,24,1536]{2,1,0:T(8,128)(2,1)S(1)} %get-tuple-element.44), channel_id=1, source_target_pairs={{0,64},{32,96},{64,0},{96,32},{1,65},{33,97},{65,1},{97,33},{2,66}... | collective-permute-start | bytes 442376 | tf_op jit(solution)/shard_map/ppermute | solution.py:173
  220.6 15.7 %collective-permute-start.14 = (bf16[2,24,1536]{2,1,0:T(8,128)(2,1)S(1)}, bf16[2,24,1536]{2,1,0:T(8,128)(2,1)S(1)}, u32[]{:S(2)}, u32[]{:S(2)}) collective-permute-start(bf16[2,24,1536]{2,1,0:T(8,128)(2,1)S(1)} %get-tuple-element.43), channel_id=1, source_target_pairs={{0,96},{32,0},{64,32},{96,64},{1,97},{33,1},{65,33},{97,65},{2,98}... | collective-permute-start | bytes 442376 | tf_op jit(solution)/shard_map/ppermute | solution.py:173
  237.9 15.1 %collective-permute-start.24 = (bf16[448,128]{1,0:T(8,128)(2,1)S(1)}, bf16[448,128]{1,0:T(8,128)(2,1)S(1)}, u32[]{:S(2)}, u32[]{:S(2)}) collective-permute-start(bf16[448,128]{1,0:T(8,128)(2,1)S(1)} %get-tuple-element.55), channel_id=1, source_target_pairs={{0,8},{8,16},{16,24},{24,0},{1,9},{9,17},{17,25},{25,1},{2,10},{10... | collective-permute-start | bytes 344072 | tf_op jit(solution)/shard_map/ppermute | solution.py:173
  238.8 14.2 %collective-permute-start.25 = (bf16[448,128]{1,0:T(8,128)(2,1)S(1)}, bf16[448,128]{1,0:T(8,128)(2,1)S(1)}, u32[]{:S(2)}, u32[]{:S(2)}) collective-permute-start(bf16[448,128]{1,0:T(8,128)(2,1)S(1)} %get-tuple-element.57), channel_id=1, source_target_pairs={{0,16},{8,24},{16,0},{24,8},{1,17},{9,25},{17,1},{25,9},{2,18},{10... | collective-permute-start | bytes 344072 | tf_op jit(solution)/shard_map/ppermute | solution.py:173
  240.7 12.4 %collective-permute-start.26 = (bf16[448,128]{1,0:T(8,128)(2,1)S(1)}, bf16[448,128]{1,0:T(8,128)(2,1)S(1)}, u32[]{:S(2)}, u32[]{:S(2)}) collective-permute-start(bf16[448,128]{1,0:T(8,128)(2,1)S(1)} %get-tuple-element.56), channel_id=1, source_target_pairs={{0,24},{8,0},{16,8},{24,16},{1,25},{9,1},{17,9},{25,17},{2,26},{10... | collective-permute-start | bytes 344072 | tf_op jit(solution)/shard_map/ppermute | solution.py:173
  241.7 16.5 %collective-permute-start.15 = (bf16[24,1536]{1,0:T(8,128)(2,1)S(1)}, bf16[24,1536]{1,0:T(8,128)(2,1)S(1)}, u32[]{:S(2)}, u32[]{:S(2)}) collective-permute-start(bf16[24,1536]{1,0:T(8,128)(2,1)S(1)} %dynamic-slice_bitcast_fusion.10), channel_id=1, source_target_pairs={{0,128},{128,0},{1,129},{129,1},{2,130},{130,2},{3,131},{131,3},{4... | collective-permute-start | bytes 221192 | tf_op jit(solution)/shard_map/ppermute | solution.py:173
  246.5 93.0 %all-to-all-start.3 = ((bf16[256,24,128]{2,1,0:T(8,128)(2,1)}), bf16[256,24,128]{2,1,0:T(8,128)(2,1)S(1)}, u32[]{:S(2)}, u32[]{:S(2)}) async-start(bf16[256,24,128]{2,1,0:T(8,128)(2,1)} %bitcast.149), calls=%async_computation.3 | async-start | bytes 3145728 | tf_op jit(solution)/shard_map/all_to_all | solution.py:213
  258.3 31.5 %collective-permute-start.16 = (bf16[24,1536]{1,0:T(8,128)(2,1)S(1)}, bf16[24,1536]{1,0:T(8,128)(2,1)S(1)}, u32[]{:S(2)}, u32[]{:S(2)}) collective-permute-start(bf16[24,1536]{1,0:T(8,128)(2,1)S(1)} %fusion.16), channel_id=1, source_target_pairs={{0,2},{2,4},{4,6},{6,0},{1,3},{3,5},{5,7},{7,1},{8,10},{10,12},{12... | collective-permute-start | bytes 221192 | tf_op jit(solution)/shard_map/ppermute | solution.py:173
  259.8 33.3 %collective-permute-start.17 = (bf16[24,1536]{1,0:T(8,128)(2,1)S(1)}, bf16[24,1536]{1,0:T(8,128)(2,1)S(1)}, u32[]{:S(2)}, u32[]{:S(2)}) collective-permute-start(bf16[24,1536]{1,0:T(8,128)(2,1)S(1)} %fusion.16), channel_id=1, source_target_pairs={{0,4},{2,6},{4,0},{6,2},{1,5},{3,7},{5,1},{7,3},{8,12},{10,14},{12... | collective-permute-start | bytes 221192 | tf_op jit(solution)/shard_map/ppermute | solution.py:173
  262.4 30.7 %collective-permute-start.18 = (bf16[24,1536]{1,0:T(8,128)(2,1)S(1)}, bf16[24,1536]{1,0:T(8,128)(2,1)S(1)}, u32[]{:S(2)}, u32[]{:S(2)}) collective-permute-start(bf16[24,1536]{1,0:T(8,128)(2,1)S(1)} %fusion.16), channel_id=1, source_target_pairs={{0,6},{2,0},{4,2},{6,4},{1,7},{3,1},{5,3},{7,5},{8,14},{10,8},{12,... | collective-permute-start | bytes 221192 | tf_op jit(solution)/shard_map/ppermute | solution.py:173
  263.4 34.8 %collective-permute-start.30 = (bf16[112,128]{1,0:T(8,128)(2,1)S(1)}, bf16[112,128]{1,0:T(8,128)(2,1)S(1)}, u32[]{:S(2)}, u32[]{:S(2)}) collective-permute-start(bf16[112,128]{1,0:T(8,128)(2,1)S(1)} %fusion.19), channel_id=1, source_target_pairs={{0,128},{128,0},{1,129},{129,1},{2,130},{130,2},{3,131},{131,3},{4... | collective-permute-start | bytes 86024 | tf_op jit(solution)/shard_map/ppermute | solution.py:173
  (31 other events, 229.7 us)
Sparse Core Ops, SparseCore 0:
  19.4 63.5 all-gather.1
